TPU v7x, 256 devices: a whole 4x4x8 slice. The times are simulated.
256 devices in a mesh: cfg: 2 (over x_lo), patch: 16 (over x_hi, y, core), head: 8 (over z).
Axes of the slice: x: 4 (x_hi: 2, x_lo: 2; x = x_hi * 2 + x_lo), y: 4, z: 8, core: 2. Of those that a mesh axis runs over, the one named last changes fastest.
Arguments:
- hidden_states: bfloat16 [2, 6144, 5120], P('cfg', 'patch'), may hold values from -6 to 6
- modulation: float32 [2, 5120], replicated, may hold values from -3 to 3
- w_query: bfloat16 [5120, 5120], P('cfg', 'head')
- w_key: bfloat16 [5120, 5120], P('cfg', 'head')
- w_value: bfloat16 [5120, 5120], P('cfg', 'head'), may hold values from -0.078125 to 0.078125
- query_gain: float32 [5120], P('head'), may hold values from 0.25 to 1.75
- key_gain: float32 [5120], P('head'), may hold values from 0.25 to 1.75
- stale_kv: bfloat16 [2, 2, 6144, 5120], P('cfg', None, 'patch', 'head'), may hold values from -6 to 6
Outputs:
- attended: bfloat16 [2, 6144, 5120], P('cfg', 'patch', 'head')
- fresh_kv: bfloat16 [2, 2, 6144, 5120], P('cfg', None, 'patch', 'head')
All inputs are finite; a program needn't handle non-finite values.
Results may differ from a plain program's by a relative error of at most 0.008.
Values may be sent and summed in bfloat16 or wider, within the bound.
A program may use at most 192 MiB of HBM per device.

v0:
```python
import jax
import jax.numpy as jnp
from jax import lax
from jax.sharding import PartitionSpec as P

HEADS = 40
HEAD_DIM = 128


def rms_parts(raw_query, raw_key):
    sums = lax.psum(
        (jnp.sum(raw_query * raw_query, axis=-1), jnp.sum(raw_key * raw_key, axis=-1)), "head"
    )
    return sums


def local(hidden_states, modulation, w_query, w_key, w_value, query_gain, key_gain, stale_kv):
    states = hidden_states[0].astype(jnp.float32)
    mean = jnp.mean(states, axis=-1, keepdims=True)
    var = jnp.mean((states - mean) ** 2, axis=-1, keepdims=True)
    normed = (
        (states - mean) * lax.rsqrt(var + 1e-06) * (1.0 + modulation[1]) + modulation[0]
    ).astype(jnp.bfloat16)
    tok_rows = normed.shape[0]
    width = w_query.shape[1]
    pieces = (
        lax.all_gather(w_query, "cfg", axis=0, tiled=True),
        lax.all_gather(w_key, "cfg", axis=0, tiled=True),
        lax.all_gather(w_value, "cfg", axis=0, tiled=True),
    )
    raw_query, raw_key, raw_value = tuple(
        (jnp.dot(normed, piece, preferred_element_type=jnp.float32) for piece in pieces)
    )
    query_sum, key_sum = rms_parts(raw_query, raw_key)
    columns_all = HEADS * HEAD_DIM
    query = (raw_query * lax.rsqrt(query_sum[:, None] / columns_all + 1e-06) * query_gain).astype(
        jnp.bfloat16
    )
    key = (raw_key * lax.rsqrt(key_sum[:, None] / columns_all + 1e-06) * key_gain).astype(
        jnp.bfloat16
    )
    value = raw_value.astype(jnp.bfloat16)
    fresh_kv = jnp.stack([key, value])[None]
    local_heads = width // HEAD_DIM
    scale = 1.0 / jnp.sqrt(jnp.float32(HEAD_DIM))
    query_heads = query.reshape(tok_rows, local_heads, HEAD_DIM)
    key_heads = key.reshape(tok_rows, local_heads, HEAD_DIM)
    value_heads = value.reshape(tok_rows, local_heads, HEAD_DIM)
    score = (
        jnp.einsum("qhd,khd->hqk", query_heads, key_heads, preferred_element_type=jnp.float32)
        * scale
    )
    top = jnp.max(score, axis=-1)
    expo = jnp.exp(score - top[:, :, None])
    total = jnp.sum(expo, axis=-1)
    summed = jnp.einsum(
        "hqk,khd->hqd", expo.astype(jnp.bfloat16), value_heads, preferred_element_type=jnp.float32
    )
    own_start = lax.axis_index("patch") * tok_rows
    piece = lax.all_gather(stale_kv[0], "patch", axis=1, tiled=True)
    count = piece.shape[1]
    keys_in = piece[0].reshape(count, local_heads, HEAD_DIM)
    values_in = piece[1].reshape(count, local_heads, HEAD_DIM)
    places = jnp.arange(count, dtype=jnp.int32)
    inside = (places >= own_start) & (places < own_start + tok_rows)
    part_score = (
        jnp.einsum("qhd,khd->hqk", query_heads, keys_in, preferred_element_type=jnp.float32) * scale
    )
    part_score = jnp.where(inside[None, None, :], jnp.float32(-1e30), part_score)
    new_top = jnp.maximum(top, jnp.max(part_score, axis=-1))
    factor = jnp.exp(top - new_top)
    part_expo = jnp.exp(part_score - new_top[:, :, None])
    new_total = total * factor + jnp.sum(part_expo, axis=-1)
    new_sum = summed * factor[:, :, None] + jnp.einsum(
        "hqk,khd->hqd",
        part_expo.astype(jnp.bfloat16),
        values_in,
        preferred_element_type=jnp.float32,
    )
    result = new_sum / new_total[:, :, None]
    attended = jnp.transpose(result, (1, 0, 2)).reshape(tok_rows, width).astype(jnp.bfloat16)
    return (attended[None], fresh_kv)


def solution(mesh):
    in_specs = (
        P("cfg", "patch", None),
        P(),
        P("cfg", "head"),
        P("cfg", "head"),
        P("cfg", "head"),
        P("head"),
        P("head"),
        P("cfg", None, "patch", "head"),
    )
    out_specs = (P("cfg", "patch", "head"), P("cfg", None, "patch", "head"))
    return jax.shard_map(local, mesh=mesh, in_specs=in_specs, out_specs=out_specs, check_vma=False)
```

profile of v0, /device:TPU:1, one launch (start us, length us, event | category | flops | bytes accessed | tf_op | source)
XLA Modules:
  0.0 494.6 jit_solution(11582549092657950141)
XLA Ops:
  7.2 0.0 copy-start.1
  7.2 0.0 all-gather.8.cloned.1.call-start
  7.2 0.7 all-gather.8.cloned.1.call-update
  7.9 0.0 all-gather.6.cloned.1.call-start
  8.0 0.7 all-gather.6.cloned.1.call-update
  8.7 0.0 copy-start.3
  8.7 0.0 all-gather.10.cloned.1.call-start
  8.7 0.7 all-gather.10.cloned.1.call-update
  9.4 0.0 all-gather.12.cloned.1.call-start
  9.4 0.0 copy-done.1
  9.5 1.3 copy.23
  10.8 0.0 all-gather.12.cloned.1.call-update
  10.8 0.0 copy-start
  10.9 2.9 convert_reduce_fusion
  13.7 3.3 fusion.9
  17.0 0.0 copy-done.3
  17.1 0.0 copy-done
  17.1 4.0 fusion.12
  21.1 81.0 %all-gather.8.cloned.1.call-done = bf16[5120,640]{1,0:T(8,128)(2,1)} async-done(((bf16[2560,640]{1,0:T(8,128)(2,1)}), bf16[5120,640]{1,0:T(8,128)(2,1)}) %all-gather.8.cloned.1.call-update) | async-done | bytes 6553616 | tf_op jit(solution)/shard_map/all_gather | solution.py:28
  102.0 7.3 %multiply_reduce_fusion.1 = (f32[384]{0:T(512)S(1)}, f32[384,640]{1,0:T(8,128)S(1)}) fusion(bf16[384,5120]{1,0:T(8,128)(2,1)} %fusion.12, bf16[5120,640]{1,0:T(8,128)(2,1)} %all-gather.8.cloned.1.call-done), kind=kOutput, calls=%fused_computation.32 | convolution fusion | flops 2517073408 | bytes 11470336 | tf_op jit(solution)/shard_map/dot_general | solution.py:32
  109.4 0.0 copy-start.5
  109.4 0.0 copy-start.4
  109.4 83.9 %all-gather.6.cloned.1.call-done = bf16[5120,640]{1,0:T(8,128)(2,1)} async-done(((bf16[2560,640]{1,0:T(8,128)(2,1)}), bf16[5120,640]{1,0:T(8,128)(2,1)}) %all-gather.6.cloned.1.call-update) | async-done | bytes 6553616 | tf_op jit(solution)/shard_map/all_gather | solution.py:27
  193.3 7.3 %multiply_reduce_fusion.2 = (f32[384]{0:T(512)S(1)}, f32[384,640]{1,0:T(8,128)S(1)}) fusion(bf16[384,5120]{1,0:T(8,128)(2,1)} %fusion.12, bf16[5120,640]{1,0:T(8,128)(2,1)} %all-gather.6.cloned.1.call-done), kind=kOutput, calls=%fused_computation.34 | convolution fusion | flops 2517073408 | bytes 11470336 | tf_op jit(solution)/shard_map/dot_general | solution.py:32
  200.6 13.9 %all-reduce = (f32[384]{0:T(512)S(1)}, f32[384]{0:T(512)S(1)}) all-reduce(f32[384]{0:T(512)S(1)} %get-tuple-element.14, f32[384]{0:T(512)S(1)} %get-tuple-element.16), channel_id=1, replica_groups=mesh['cfg'=2,'patch'=16,'head'=8] {'head'}, use_global_device_ids=true, to_apply=%region_3.0 | all-reduce | flops 768 | bytes 6144 | tf_op jit(solution)/shard_map/psum | solution.py:11
  214.5 0.0 copy-done.5
  214.5 0.2 multiply_convert_fusion.1
  214.7 0.3 copy.17
  214.9 0.0 copy-done.4
  214.9 0.2 multiply_convert_fusion
  215.1 1.0 copy.18
  216.1 68.4 %all-gather.10.cloned.1.call-done = bf16[5120,640]{1,0:T(8,128)(2,1)} async-done(((bf16[2560,640]{1,0:T(8,128)(2,1)}), bf16[5120,640]{1,0:T(8,128)(2,1)}) %all-gather.10.cloned.1.call-update) | async-done | bytes 6553616 | tf_op jit(solution)/shard_map/all_gather | solution.py:29
  284.5 7.3 %convolution_convert_fusion = bf16[384,640]{1,0:T(8,128)(2,1)S(1)} fusion(bf16[384,5120]{1,0:T(8,128)(2,1)} %fusion.12, bf16[5120,640]{1,0:T(8,128)(2,1)} %all-gather.10.cloned.1.call-done), kind=kOutput, calls=%fused_computation.27 | convolution fusion | flops 2516828160 | bytes 10977280 | tf_op jit(solution)/shard_map/dot_general | solution.py:32
  291.8 1.0 copy.21
  292.8 0.2 fusion.56
  292.9 1.1 maximum_bitcast_fusion
  294.0 1.6 multiply_reduce_fusion
  295.6 0.5 fusion.13
  296.1 111.0 %all-gather.12.cloned.1.call-done = bf16[1,2,6144,640]{2,3,1,0:T(8,128)(2,1)} async-done(((bf16[1,2,384,640]{2,3,1,0:T(8,128)(2,1)}), bf16[1,2,6144,640]{2,3,1,0:T(8,128)(2,1)}) %all-gather.12.cloned.1.call-update) | async-done | bytes 15728656 | tf_op jit(solution)/shard_map/all_gather | solution.py:60
  407.1 11.3 %fusion.43 = (bf16[1,1,6144,640]{2,3,1,0:T(8,128)(2,1)}, bf16[1,1,6144,640]{2,3,1,0:T(8,128)(2,1)}) fusion(bf16[1,2,6144,640]{2,3,1,0:T(8,128)(2,1)} %all-gather.12.cloned.1.call-done), kind=kLoop, calls=%fused_computation.50 | loop fusion | bytes 31457280 | tf_op jit(solution)/shard_map/slice | solution.py:62
  418.3 21.5 %fusion = (f32[5,384]{1,0:T(8,128)S(1)}, f32[5,384,6144]{2,1,0:T(8,128)}) fusion(pred[6144]{0:T(1024)(128)(4,1)S(1)} %fusion.37, bf16[384,5,128]{0,2,1:T(8,128)(2,1)S(1)} %bitcast.68, bf16[6144,5,128]{0,2,1:T(8,128)(2,1)} %bitcast.65), kind=kOutput, calls=%fused_computation.2 | convolution fusion | flops 3055286272 | bytes 55555584 | tf_op jit(solution)/shard_map/qhd,khd->hqk/dot_general | solution.py:67
  439.8 20.3 %fusion.1 = f32[5,384]{1,0:T(8,128)S(1)} fusion(f32[5,384,6144]{2,1,0:T(8,128)} %get-tuple-element.21, f32[5,384]{1,0:T(8,128)S(1)} %max.18, pred[6144]{0:T(1024)(128)(4,1)S(1)} %fusion.37), kind=kLoop, calls=%fused_computation.3 | loop fusion | flops 47184000 | bytes 47207424 | tf_op jit(solution)/shard_map/reduce_sum | solution.py:73
  460.2 0.0 copy-start.2
  460.2 23.1 %fusion.28 = f32[384,5,128]{0,2,1:T(8,128)} fusion(bf16[6144,5,128]{0,2,1:T(8,128)(2,1)} %bitcast.66, f32[5,384,6144]{2,1,0:T(8,128)} %get-tuple-element.21, f32[5,384]{1,0:T(8,128)S(1)} %max.18, pred[6144]{0:T(1024)(128)(4,1)S(1)} %fusion.37), kind=kOutput, calls=%fused_computation.26 | convolution fusion | flops 3067084800 | bytes 56047104 | tf_op jit(solution)/shard_map/hqk,khd->hqd/dot_general | solution.py:74
  483.3 0.0 copy-done.2
  483.3 2.8 fusion.34
  486.1 2.0 copy.26
  (7 shorter events, 0.1 us)
Async XLA Ops:
  7.2 2.3 copy-start.1
  7.2 94.9 %all-gather.8.cloned.1.call-start = ((), (), s32[]{:S(2)}) async-start(), calls=%async_computation.1 | async-start | bytes 9830400 | tf_op jit(solution)/shard_map/all_gather | solution.py:28
  7.9 185.4 %all-gather.6.cloned.1.call-start = ((), (), s32[]{:S(2)}) async-start(), calls=%async_computation | async-start | bytes 9830400 | tf_op jit(solution)/shard_map/all_gather | solution.py:27
  8.7 8.4 %copy-start.3 = (f32[2,5120]{1,0:T(2,128)S(1)}, f32[2,5120]{1,0:T(2,128)}, u32[]{:S(2)}) copy-start(f32[2,5120]{1,0:T(2,128)} %param.9) | copy-start | bytes 122884
  8.7 275.8 %all-gather.10.cloned.1.call-start = ((), (), s32[]{:S(2)}) async-start(), calls=%async_computation.2 | async-start | bytes 9830400 | tf_op jit(solution)/shard_map/all_gather | solution.py:29
  9.4 397.7 %all-gather.12.cloned.1.call-start = ((), (), s32[]{:S(2)}) async-start(), calls=%async_computation.3 | async-start | bytes 16711680 | tf_op jit(solution)/shard_map/all_gather | solution.py:60
  10.8 6.2 %copy-start = (bf16[1,384,5120]{2,1,0:T(8,128)(2,1)S(1)}, bf16[1,384,5120]{2,1,0:T(8,128)(2,1)}, u32[]{:S(2)}) copy-start(bf16[1,384,5120]{2,1,0:T(8,128)(2,1)} %param.8) | copy-start | bytes 11796484
  109.4 105.1 %copy-start.5 = (f32[640]{0:T(1024)S(1)}, f32[640]{0:T(1024)}, u32[]{:S(2)}) copy-start(f32[640]{0:T(1024)} %param.13) | copy-start | bytes 7684
  109.4 105.6 %copy-start.4 = (f32[640]{0:T(1024)S(1)}, f32[640]{0:T(1024)}, u32[]{:S(2)}) copy-start(f32[640]{0:T(1024)} %param.14) | copy-start | bytes 7684
  460.2 23.2 %copy-start.2 = (bf16[384,640]{0,1:T(8,128)(2,1)S(1)}, bf16[384,640]{0,1:T(8,128)(2,1)}, u32[]{:S(2)}) copy-start(bf16[384,640]{0,1:T(8,128)(2,1)} %copy.21) | copy-start | bytes 1474564
Sparse Core Ops, SparseCore 0:
  9.8 92.1 all-gather.7
  103.8 89.3 all-gather.5
  195.1 89.3 all-gather.9
  286.9 120.1 all-gather.11
where the time goes:
time: 495 us
  waiting for transfers between devices  346 us (70%)
  matrix products  70.9 us (14%)
  other arithmetic  32.6 us (7%)
  local copies, waits for them, and re-layouts  16.9 us (3%)
  blocking collectives  13.9 us (3%)
  between operations  13.9 us (3%)
    all_gather x1, waiting for transfers between devices, local(): piece = lax.all_gather(stale_kv[0], 'patch', axis=1, tiled=True)  111 us
    all_gather x1, waiting for transfers between devices, local(): lax.all_gather(w_query, 'cfg', axis=0, tiled=True)  83.9 us
    all_gather x1, waiting for transfers between devices, local(): lax.all_gather(w_key, 'cfg', axis=0, tiled=True)  81 us
    all_gather x1, waiting for transfers between devices, local(): lax.all_gather(w_value, 'cfg', axis=0, tiled=True)  68.4 us
    dot_general x1, matrix products, local(): jnp.einsum('hqk,khd->hqd', part_expo.astype(jnp.bfloat16), values_in, pre...  23.1 us
    dot_general x3, matrix products, local(): jnp.dot(normed, piece, preferred_element_type=jnp.float32)  21.9 us
    dot_general x1, matrix products, local(): jnp.einsum('qhd,khd->hqk', query_heads, keys_in, preferred_element_type=j...  21.5 us
    reduce_sum x1, other arithmetic, local(): new_total = total * factor + jnp.sum(part_expo, axis=-1)  20.3 us
  transfers between devices with their start and end apart: 4, of which 4 were waited for; matrix products, arithmetic and copies ran while one was open for 8% of the time, Pallas kernels for 0%

commit v1 on v0

v1 whole, which is shorter than its diff:
```python
import functools

import jax
import jax.numpy as jnp
from jax import lax
from jax.experimental import pallas as pl
from jax.experimental.pallas import tpu as pltpu
from jax.sharding import PartitionSpec as P

HEAD_DIM = 128
SCORE_SCALE = 1.4426950408889634 / 128.0**0.5
LOW = -1e30
MESH = pl.DeviceIdType.MESH
F32 = jnp.float32
BF16 = jnp.bfloat16


def kernel(
    n_head, columns_all,
    hid_any, mod, wq_any, wk_any, wv_any, gain_q, gain_k, stale_any,
    att_out, fresh,
    hid, nrm, wown, woth, raw, kvs, qs, top, acc, o_send, o_recv, lse_send, lse_recv, zs,
    ld, wps, wpr, wss, wsr, kys, kyr, k3s, k3r, kss, ksr, qss, qsr, oss, osr, zss, zsr,
):
    tok = hid.shape[0]
    depth = wown.shape[1]
    width = wown.shape[2]
    heads = width // HEAD_DIM
    quarter = depth // 4
    part = quarter // 2
    half = tok // 2

    c = lax.axis_index("cfg")
    p = lax.axis_index("patch")
    h = lax.axis_index("head")
    core = p % 2
    y = (p // 2) % 4
    xh = p // 8

    def at(xh_, y_, core_):
        return (xh_ * 4 + y_) * 2 + core_

    SIB = (c, at(xh, y, 1 - core), h)
    XD = (1 - c, p, h)
    XO = (1 - c, at(1 - xh, y, core), h)
    X2 = (c, at(1 - xh, y, core), h)
    YP = (c, at(xh, (y + 1) % 4, core), h)
    YM = (c, at(xh, (y + 3) % 4, core), h)
    ZS = [(c, p, (h + d) % n_head) for d in range(1, n_head)]
    w_any = (wq_any, wk_any, wv_any)

    loads = [
        pltpu.make_async_copy(hid_any.at[0], hid, ld.at[0]),
        pltpu.make_async_copy(wq_any, wown.at[0], ld.at[1]),
        pltpu.make_async_copy(wk_any, wown.at[1], ld.at[2]),
        pltpu.make_async_copy(wv_any, wown.at[2], ld.at[3]),
        pltpu.make_async_copy(stale_any.at[0], kvs.at[0, :, pl.ds(0, tok)], ld.at[4]),
    ]

    barrier = pltpu.get_barrier_semaphore()
    partners = [SIB, XD, XO, X2, YP, YM] + ZS
    for device in partners:
        pl.semaphore_signal(barrier, inc=1, device_id=device, device_id_type=MESH)
    for load in loads:
        load.start()
    pl.semaphore_wait(barrier, len(partners))

    sent = []

    def send(src, dst, ss, rs, device):
        copy = pltpu.make_async_remote_copy(
            src_ref=src, dst_ref=dst, send_sem=ss, recv_sem=rs, device_id=device, device_id_type=MESH
        )
        copy.start()
        return copy

    def pending(describe):
        sent.append(describe)

    def arrived(dst, rs):
        pltpu.make_async_remote_copy(
            src_ref=dst, dst_ref=dst, send_sem=rs, recv_sem=rs, device_id=SIB, device_id_type=MESH
        ).wait_recv()

    def quarter_of(d):
        return (y + d) % 4

    def piece(d, side):
        return pl.ds(pl.multiple_of(quarter_of(d) * quarter + side * part, 16), part)

    def whole(d):
        return pl.ds(pl.multiple_of(quarter_of(d) * quarter, 16), quarter)

    def weight_x(m, d, device):
        rows = piece(d, core)
        send(w_any[m].at[rows], woth.at[m, rows], wps.at[m, d], wpr.at[m, d], device)
        pending(lambda: (w_any[m].at[piece(d, core)], wps.at[m, d]))

    def weight_sib(m, d):
        rows = piece(d, core)
        arrived(woth.at[m, rows], wpr.at[m, d])
        send(woth.at[m, rows], woth.at[m, rows], wss.at[m, d], wsr.at[m, d], SIB)
        pending(lambda: (woth.at[m, piece(d, core)], wss.at[m, d]))

    def weight_y(m):
        rows = piece(0, core)
        for d, device in ((3, YP), (1, YM)):
            send(woth.at[m, rows], woth.at[m, rows], wps.at[m, d], wpr.at[m, d], device)
            pending(lambda d=d: (woth.at[m, piece(0, core)], wps.at[m, d]))

    def weight_dot(m, d):
        arrived(woth.at[m, piece(d, 1 - core)], wsr.at[m, d])
        lanes = pl.ds(pl.multiple_of((1 - c) * depth + quarter_of(d) * quarter, 128), quarter)
        raw[m] += jnp.dot(nrm[:, lanes], woth[m, whole(d), :], preferred_element_type=F32)

    mine = pl.ds(0, tok)
    other = pl.ds(tok, tok)

    def kv_out(i):
        src = stale_any.at[0, i]
        send(src, kvs.at[2, i, mine], kys.at[0, i], kyr.at[1, i], YP)
        send(src, kvs.at[1, i, mine], kys.at[1, i], kyr.at[0, i], YM)
        send(src, kvs.at[0, i, other], kss.at[0, i], ksr.at[0, i], SIB)
        pending(lambda: (stale_any.at[0, i], kys.at[0, i]))
        pending(lambda: (stale_any.at[0, i], kys.at[1, i]))
        pending(lambda: (stale_any.at[0, i], kss.at[0, i]))

    def kv_sib(slot, i):
        send(kvs.at[slot, i, mine], kvs.at[slot, i, other], kss.at[slot, i], ksr.at[slot, i], SIB)
        pending(lambda: (kvs.at[slot, i, pl.ds(0, tok)], kss.at[slot, i]))

    def kv_forward(i):
        for k, device in ((0, YM), (1, YP)):
            rows = pl.ds(k * half, half)
            arrived(kvs.at[1 + k, i, mine], kyr.at[k, i])
            send(kvs.at[1 + k, i, rows], kvs.at[3, i, rows], k3s.at[k, i], k3r.at[k, i], device)
            pending(lambda k=k: (kvs.at[1 + k, i, pl.ds(k * half, half)], k3s.at[k, i]))
            kv_sib(1 + k, i)

    def kv_last(i):
        for k in range(2):
            arrived(kvs.at[3, i, pl.ds(k * half, half)], k3r.at[k, i])
        kv_sib(3, i)

    def kv_ready(slot):
        for i in range(2):
            arrived(kvs.at[slot, i, other], ksr.at[slot, i])

    def squares_out(k, m):
        r = raw[m]
        column = jnp.sum(r * r, axis=1, keepdims=True)
        zs[k, 0] = jnp.transpose(jnp.broadcast_to(column, (tok, 128)))[:8, :]
        for d in range(1, n_head):
            send(zs.at[k, 0], zs.at[k, d], zss.at[k, d - 1], zsr.at[k, d - 1], ZS[d - 1])
            pending(lambda d=d: (zs.at[k, 0], zss.at[k, d - 1]))

    def normalised(k, m, gain):
        total = zs[k, 0]
        for d in range(1, n_head):
            arrived(zs.at[k, d], zsr.at[k, d - 1])
            total = total + zs[k, d]
        factor = lax.rsqrt(total / columns_all + 1e-06)
        factor = jnp.transpose(jnp.broadcast_to(factor[:1, :], (128, tok)))
        return [
            (raw[m, :, j * 128 : (j + 1) * 128] * factor * gain[:, j * 128 : (j + 1) * 128]).astype(BF16)
            for j in range(heads)
        ]

    tiles = 3 if tok % 48 == 0 else 1
    step = tok // tiles

    def attend(s, key_ref, value_ref):
        for j in range(heads):
            lanes = slice(j * 128, (j + 1) * 128)
            for t in range(tiles):
                rows = slice(t * step, (t + 1) * step)
                key = key_ref[:, lanes]
                value = value_ref[:, lanes]
                score = lax.dot_general(
                    qs[s, rows, lanes], key, (((1,), (1,)), ((), ())), preferred_element_type=F32
                )
                score = score * SCORE_SCALE
                before = top[s, j, rows, :]
                now = jnp.maximum(before, jnp.max(score, axis=1, keepdims=True))
                shrink = jnp.exp2(before - now)
                weight = jnp.exp2(score - now[:, :1]).astype(BF16)
                added = jnp.dot(
                    weight, jnp.concatenate([value, jnp.ones_like(value)], axis=1), preferred_element_type=F32
                )
                acc[s, j, rows, :] = acc[s, j, rows, :] * jnp.concatenate([shrink, shrink], axis=1) + added
                top[s, j, rows, :] = now

    weight_x(0, 0, XD)
    weight_x(0, 2, XO)
    kv_out(0)

    loads[0].wait()

    def norm_rows(i, carry):
        rows = pl.ds(pl.multiple_of(i * 16, 16), 16)
        states = hid[rows, :].astype(F32)
        mean = jnp.mean(states, axis=1, keepdims=True)
        states = states - mean
        var = jnp.mean(states * states, axis=1, keepdims=True)
        nrm[rows, :] = (states * lax.rsqrt(var + 1e-06) * (1.0 + mod[1:2, :]) + mod[0:1, :]).astype(BF16)
        return carry

    lax.fori_loop(0, tok // 16, norm_rows, 0)
    weight_x(0, 1, XD)
    weight_x(0, 3, XO)
    kv_out(1)

    for load in loads[1:4]:
        load.wait()
    own_lanes = pl.ds(pl.multiple_of(c * depth, 128), depth)

    def own_dot(m, carry):
        raw[m] = jnp.dot(nrm[:, own_lanes], wown[m], preferred_element_type=F32)
        return carry

    lax.fori_loop(0, 3, own_dot, 0)

    weight_sib(0, 0)
    weight_sib(0, 2)
    kv_forward(0)
    top[...] = jnp.full_like(top, LOW)
    acc[...] = jnp.zeros_like(acc)
    weight_dot(0, 0)
    weight_dot(0, 2)
    weight_sib(0, 1)
    weight_sib(0, 3)
    weight_x(1, 0, XD)
    weight_x(1, 2, XO)
    weight_dot(0, 1)
    weight_dot(0, 3)
    squares_out(0, 0)
    kv_forward(1)
    for j, head in enumerate(normalised(0, 0, gain_q)):
        qs[0, :, j * 128 : (j + 1) * 128] = head
    send(qs.at[0], qs.at[1], qss.at[0], qsr.at[0], X2)
    pending(lambda: (qs.at[0], qss.at[0]))

    loads[4].wait()
    kv_ready(0)
    attend(0, kvs.at[0, 0, other], kvs.at[0, 1, other])

    def unit(i, carry):
        s = (i + 1) // 4
        j = (i + 1) % 4

        @pl.when(i == 0)
        def _():
            kv_ready(1)

        @pl.when(i == 1)
        def _():
            weight_sib(1, 0)
            weight_sib(1, 2)
            weight_y(1)
            weight_x(2, 0, XD)
            weight_x(2, 2, XO)
            kv_ready(2)

        @pl.when(i == 2)
        def _():
            kv_last(0)
            kv_last(1)
            kv_ready(3)

        @pl.when(i == 3)
        def _():
            arrived(qs.at[1], qsr.at[0])

        @pl.when(i == 4)
        def _():
            weight_sib(1, 1)
            weight_sib(1, 3)
            for d in (0, 2, 1, 3):
                weight_dot(1, d)
            squares_out(1, 1)

        @pl.when(i == 5)
        def _():
            weight_sib(2, 0)
            weight_sib(2, 2)
            weight_y(2)

        @pl.when(i == 6)
        def _():
            for k, head in enumerate(normalised(1, 1, gain_k)):
                fresh[0, 0, :, k * 128 : (k + 1) * 128] = head
            weight_dot(2, 0)
            weight_dot(2, 2)

        attend(s, kvs.at[j, 0], kvs.at[j, 1])
        return carry

    lax.fori_loop(0, 7, unit, 0)

    lane = lax.broadcasted_iota(jnp.int32, (tok, 128), 1)
    packed = jnp.zeros((tok, 128), F32)
    for j in range(heads):
        total = acc[1, j, :, 128:]
        o_send[:, j * 128 : (j + 1) * 128] = (acc[1, j, :, :128] / total).astype(BF16)
        packed = jnp.where(lane == j, top[1, j] + jnp.log2(total), packed)
    lse_send[...] = jnp.transpose(packed)[:8, :]
    send(lse_send, lse_recv, oss.at[1], osr.at[1], X2)
    pending(lambda: (lse_send, oss.at[1]))
    send(o_send, o_recv, oss.at[0], osr.at[0], X2)
    pending(lambda: (o_send, oss.at[0]))

    weight_sib(2, 1)
    weight_sib(2, 3)
    weight_dot(2, 1)
    weight_dot(2, 3)
    fresh[0, 1] = raw[2].astype(BF16)
    attend(0, fresh.at[0, 0], fresh.at[0, 1])

    arrived(lse_recv, osr.at[1])
    arrived(o_recv, osr.at[0])
    far = jnp.transpose(jnp.concatenate([lse_recv[...]] * 16, axis=0))
    for j in range(heads):
        lanes = slice(j * 128, (j + 1) * 128)
        near = top[0, j]
        there = jnp.broadcast_to(far[:, j : j + 1], (tok, 128))
        highest = jnp.maximum(near, there)
        a = jnp.exp2(near - highest)
        b = jnp.exp2(there - highest)
        summed = acc[0, j, :, :128] * a + o_recv[:, lanes].astype(F32) * b
        att_out[0, :, lanes] = (summed / (acc[0, j, :, 128:] * a + b)).astype(BF16)

    for describe in sent:
        src, ss = describe()
        pltpu.make_async_remote_copy(
            src_ref=src, dst_ref=src, send_sem=ss, recv_sem=ss, device_id=SIB, device_id_type=MESH
        ).wait_send()


def local(n_head, hidden_states, modulation, w_query, w_key, w_value, query_gain, key_gain, stale_kv):
    tok = hidden_states.shape[1]
    depth, width = w_query.shape
    heads = width // HEAD_DIM
    hbm = pl.BlockSpec(memory_space=pl.ANY)
    vmem = pl.BlockSpec(memory_space=pltpu.VMEM)
    dma = pltpu.SemaphoreType.DMA
    peers = max(n_head - 1, 1)
    return pl.pallas_call(
        functools.partial(kernel, n_head, float(n_head * width)),
        out_shape=(
            jax.ShapeDtypeStruct((1, tok, width), BF16),
            jax.ShapeDtypeStruct((1, 2, tok, width), BF16),
        ),
        in_specs=[hbm, vmem, hbm, hbm, hbm, vmem, vmem, hbm],
        out_specs=(vmem, vmem),
        scratch_shapes=[
            pltpu.VMEM((tok, 2 * depth), BF16),
            pltpu.VMEM((tok, 2 * depth), BF16),
            pltpu.VMEM((3, depth, width), BF16),
            pltpu.VMEM((3, depth, width), BF16),
            pltpu.VMEM((3, tok, width), F32),
            pltpu.VMEM((4, 2, 2 * tok, width), BF16),
            pltpu.VMEM((2, tok, width), BF16),
            pltpu.VMEM((2, heads, tok, 128), F32),
            pltpu.VMEM((2, heads, tok, 256), F32),
            pltpu.VMEM((tok, width), BF16),
            pltpu.VMEM((tok, width), BF16),
            pltpu.VMEM((8, tok), F32),
            pltpu.VMEM((8, tok), F32),
            pltpu.VMEM((2, n_head, 8, tok), F32),
            dma((5,)),
            dma((3, 4)), dma((3, 4)), dma((3, 4)), dma((3, 4)),
            dma((2, 2)), dma((2, 2)), dma((2, 2)), dma((2, 2)), dma((4, 2)), dma((4, 2)),
            dma((1,)), dma((1,)), dma((2,)), dma((2,)), dma((2, peers)), dma((2, peers)),
        ],
        compiler_params=pltpu.CompilerParams(
            collective_id=0, has_side_effects=True, vmem_limit_bytes=60 * 2**20
        ),
    )(
        hidden_states, modulation, w_query, w_key, w_value,
        query_gain.reshape(1, width), key_gain.reshape(1, width), stale_kv,
    )


def solution(mesh):
    in_specs = (
        P("cfg", "patch", None),
        P(),
        P("cfg", "head"),
        P("cfg", "head"),
        P("cfg", "head"),
        P("head"),
        P("head"),
        P("cfg", None, "patch", "head"),
    )
    out_specs = (P("cfg", "patch", "head"), P("cfg", None, "patch", "head"))
    run = functools.partial(local, mesh.shape["head"])
    return jax.shard_map(run, mesh=mesh, in_specs=in_specs, out_specs=out_specs, check_vma=False)
```

time: 495 us -> 95.6 us (0.19)
  the two profiles are of different devices: /device:TPU:1 before, /device:TPU:2 now
where the time goes in v1:
time: 95.6 us; the launch traced here: 95.3 us
  Pallas kernels  88 us (92%)
  local copies, waits for them, and re-layouts  6.61 us (7%)
    pallas_call x1, Pallas kernels, local(): pl.pallas_call(functools.partial(kernel, n_head, float(n_head * width)),...  88 us
    unnamed x2, local copies, waits for them, and re-layouts  4.08 us

profile of v1, /device:TPU:2, one launch (start us, length us, event | category | flops | bytes accessed | tf_op | source)
XLA Modules:
  0.0 95.3 jit_solution(1572520378304191555)
XLA Ops:
  0.6 1.3 %reshape.10.gain_q = f32[1,640]{1,0:T(1,128)} reshape(f32[640]{0:T(1024)} %param.13) | data formatting | bytes 5120 | tf_op jit(solution)/shard_map/reshape | solution.py:380
  1.9 1.3 %reshape.11.gain_k = f32[1,640]{1,0:T(1,128)} reshape(f32[640]{0:T(1024)} %param.14) | data formatting | bytes 5120 | tf_op jit(solution)/shard_map/reshape | solution.py:380
  3.2 88.0 %shard_map.95 = (bf16[1,384,640]{2,1,0:T(8,128)(2,1)}, bf16[1,2,384,640]{3,2,1,0:T(8,128)(2,1)}) custom-call(bf16[1,384,5120]{2,1,0:T(8,128)(2,1)} %hid_any.1, f32[2,5120]{1,0:T(2,128)} %mod.1, bf16[2560,640]{1,0:T(8,128)(2,1)} %wq_any.1, bf16[2560,640]{1,0:T(8,128)(2,1)} %wk_any.1, bf16[2560,640]{1,0:T(8,128)(2,1)} %wv_any.1, f32[1,640]{1,0:T(1,128)} %reshape.10.gain_q, ...), custom_call_target="tpu_custom_call" | custom-call | tf_op jit(solution)/shard_map/pallas_call | solution.py:347
  91.2 1.9 %copy.12 = bf16[1,384,640]{2,1,0:T(8,128)(2,1)} copy(bf16[1,384,640]{2,1,0:T(8,128)(2,1)} %get-tuple-element.4) | data formatting | bytes 983040
  93.0 2.2 %copy.13 = bf16[1,2,384,640]{3,2,1,0:T(8,128)(2,1)} copy(bf16[1,2,384,640]{3,2,1,0:T(8,128)(2,1)} %get-tuple-element.5) | data formatting | bytes 1966080

commit v2 on v1

v2 whole, which is shorter than its diff:
```python
import functools

import jax
import jax.numpy as jnp
from jax import lax
from jax.experimental import pallas as pl
from jax.experimental.pallas import tpu as pltpu
from jax.sharding import PartitionSpec as P

HEAD_DIM = 128
SCORE_SCALE = 1.4426950408889634 / 128.0**0.5
LOW = -1e30
SHARE3 = (True, False, False)
MESH = pl.DeviceIdType.MESH
F32 = jnp.float32
BF16 = jnp.bfloat16


def kernel(
    n_head, columns_all,
    hid_any, mod, wq_any, wk_any, wv_any, gain_q, gain_k, stale_any,
    att_out, fresh_out,
    att, fresh, hid, nrm, wown, woth, raw, kvs, qs, fac, fac_rows, top, acc, o_send, o_recv, lse, lse_send, lse_recv, zs,
    ld, wps, wpr, wss, wsr, kys, kyr, k3s, k3r, kss, ksr, qss, qsr, oss, osr, zss, zsr,
):
    tok = hid.shape[0]
    depth = wown.shape[1]
    width = wown.shape[2]
    heads = width // HEAD_DIM
    quarter = depth // 4
    part = quarter // 4
    half = tok // 2
    blocks = tok // 128

    c = lax.axis_index("cfg")
    p = lax.axis_index("patch")
    h = lax.axis_index("head")
    core = p % 2
    y = (p // 2) % 4
    xh = p // 8

    def at(xh_, y_, core_):
        return (xh_ * 4 + y_) * 2 + core_

    SIB = (c, at(xh, y, 1 - core), h)
    XD = (1 - c, p, h)
    XO = (1 - c, at(1 - xh, y, core), h)
    X2 = (c, at(1 - xh, y, core), h)
    YP = (c, at(xh, (y + 1) % 4, core), h)
    YM = (c, at(xh, (y + 3) % 4, core), h)
    ZS = [(c, p, (h + d) % n_head) for d in range(1, n_head)]
    w_any = (wq_any, wk_any, wv_any)

    loads = [
        pltpu.make_async_copy(hid_any.at[0], hid, ld.at[0]),
        pltpu.make_async_copy(wq_any, wown.at[0], ld.at[1]),
        pltpu.make_async_copy(wk_any, wown.at[1], ld.at[2]),
        pltpu.make_async_copy(wv_any, wown.at[2], ld.at[3]),
        pltpu.make_async_copy(stale_any.at[0], kvs.at[0, :, pl.ds(0, tok)], ld.at[4]),
    ]

    barrier = pltpu.get_barrier_semaphore()
    partners = [SIB, XD, XO, X2, YP, YM] + ZS
    for device in partners:
        pl.semaphore_signal(barrier, inc=1, device_id=device, device_id_type=MESH)
    for load in loads:
        load.start()
    pl.semaphore_wait(barrier, len(partners))

    sent = []

    def send(src, dst, ss, rs, device):
        copy = pltpu.make_async_remote_copy(
            src_ref=src, dst_ref=dst, send_sem=ss, recv_sem=rs, device_id=device, device_id_type=MESH
        )
        copy.start()
        return copy

    def pending(describe):
        sent.append(describe)

    def arrived(dst, rs):
        pltpu.make_async_remote_copy(
            src_ref=dst, dst_ref=dst, send_sem=rs, recv_sem=rs, device_id=SIB, device_id_type=MESH
        ).wait_recv()

    def quarter_of(d):
        return (y + d) % 4

    def piece(d, e, side):
        return pl.ds(pl.multiple_of(quarter_of(d) * quarter + (2 * side + e) * part, 16), part)

    def whole(d):
        return pl.ds(pl.multiple_of(quarter_of(d) * quarter, 16), quarter)

    def weight_x(m, d, e, device):
        rows = piece(d, e, core)
        send(w_any[m].at[rows], woth.at[m, rows], wps.at[m, d, e], wpr.at[m, d, e], device)
        pending(lambda: (w_any[m].at[piece(d, e, core)], wps.at[m, d, e]))

    def weight_first(m):
        for e in range(2):
            weight_x(m, 0, e, XD)
            weight_x(m, 2, e, XO)

    def weight_third(m):
        weight_x(m, 1, 0, XD)
        weight_x(m, 1, 1, XO)

    def weight_y(m, d, e, to_d, device):
        rows = piece(d, e, core)
        send(woth.at[m, rows], woth.at[m, rows], wps.at[m, to_d, e], wpr.at[m, to_d, e], device)
        pending(lambda: (woth.at[m, piece(d, e, core)], wps.at[m, to_d, e]))

    def weight_sib(m, d, e):
        rows = piece(d, e, core)
        arrived(woth.at[m, rows], wpr.at[m, d, e])
        send(woth.at[m, rows], woth.at[m, rows], wss.at[m, d, e], wsr.at[m, d, e], SIB)
        pending(lambda: (woth.at[m, piece(d, e, core)], wss.at[m, d, e]))

    def weight_on(m, e):
        weight_sib(m, 0, e)
        weight_sib(m, 2, e)
        if e == 0:
            weight_y(m, 0, 0, 3, YP)
            if not SHARE3[m]:
                weight_y(m, 0, 0, 1, YM)
        else:
            weight_y(m, 2, 1, 3, YM)
            if not SHARE3[m]:
                weight_y(m, 2, 1, 1, YP)

    def weight_rest(m):
        for d in (1, 3):
            for e in range(2):
                weight_sib(m, d, e)

    def weight_dot(m, d):
        for e in range(2):
            arrived(woth.at[m, piece(d, e, 1 - core)], wsr.at[m, d, e])
        lanes = pl.ds(pl.multiple_of((1 - c) * depth + quarter_of(d) * quarter, 128), quarter)
        raw[m] += jnp.dot(nrm[:, lanes], woth[m, whole(d), :], preferred_element_type=F32)

    mine = pl.ds(0, tok)
    other = pl.ds(tok, tok)

    def kv_out(i):
        src = stale_any.at[0, i]
        send(src, kvs.at[2, i, mine], kys.at[0, i], kyr.at[1, i], YP)
        send(src, kvs.at[1, i, mine], kys.at[1, i], kyr.at[0, i], YM)
        send(src, kvs.at[0, i, other], kss.at[0, i], ksr.at[0, i], SIB)
        pending(lambda: (stale_any.at[0, i], kys.at[0, i]))
        pending(lambda: (stale_any.at[0, i], kys.at[1, i]))
        pending(lambda: (stale_any.at[0, i], kss.at[0, i]))

    def kv_sib(slot, i):
        send(kvs.at[slot, i, mine], kvs.at[slot, i, other], kss.at[slot, i], ksr.at[slot, i], SIB)
        pending(lambda: (kvs.at[slot, i, pl.ds(0, tok)], kss.at[slot, i]))

    def kv_forward(i):
        for k, device in ((0, YM), (1, YP)):
            rows = pl.ds(k * half, half)
            arrived(kvs.at[1 + k, i, mine], kyr.at[k, i])
            send(kvs.at[1 + k, i, rows], kvs.at[3, i, rows], k3s.at[k, i], k3r.at[k, i], device)
            pending(lambda k=k: (kvs.at[1 + k, i, pl.ds(k * half, half)], k3s.at[k, i]))
            kv_sib(1 + k, i)

    def kv_last(i):
        for k in range(2):
            arrived(kvs.at[3, i, pl.ds(k * half, half)], k3r.at[k, i])
        kv_sib(3, i)

    def kv_ready(slot):
        for i in range(2):
            arrived(kvs.at[slot, i, other], ksr.at[slot, i])

    def squares_out(k, m):
        r = raw[m]
        column = jnp.broadcast_to(jnp.sum(r * r, axis=1, keepdims=True), (tok, 128))
        zs[k, 0] = jnp.zeros((8, 128), F32)
        for i in range(blocks):
            zs[k, 0, i : i + 1, :] = jnp.transpose(column[i * 128 : (i + 1) * 128])[:1, :]
        for d in range(1, n_head):
            send(zs.at[k, 0], zs.at[k, d], zss.at[k, d - 1], zsr.at[k, d - 1], ZS[d - 1])
            pending(lambda d=d: (zs.at[k, 0], zss.at[k, d - 1]))

    def norm_factor(k):
        total = zs[k, 0]
        for d in range(1, n_head):
            arrived(zs.at[k, d], zsr.at[k, d - 1])
            total = total + zs[k, d]
        return lax.rsqrt(total / columns_all + 1e-06)

    def column_of(rows, i):
        return jnp.transpose(jnp.broadcast_to(rows[i : i + 1, :], (128, 128)))

    def spread(s):
        rows = fac_rows[s]
        for i in range(blocks):
            fac[s, i * 128 : (i + 1) * 128, :] = column_of(rows, i)

    def head_gain(gain, j):
        return gain[j * 128 : (j + 1) * 128][None, :]

    def wide(v, keys):
        return jnp.concatenate([v] * (keys // 128), axis=1)

    tiles = 3 if tok % 48 == 0 else 1
    step = tok // tiles

    def attend(key_ref, value_ref):
        keys = key_ref.shape[0]
        for j in range(heads):
            lanes = slice(j * 128, (j + 1) * 128)
            for t in range(tiles):
                rows = slice(t * step, (t + 1) * step)
                value = value_ref[:, lanes]
                score = lax.dot_general(
                    qs[0, rows, lanes], key_ref[:, lanes], (((1,), (1,)), ((), ())), preferred_element_type=F32
                )
                score = score * wide(fac[0, rows, :], keys)
                before = top[j, rows, :]
                now = jnp.maximum(before, jnp.max(score, axis=1, keepdims=True))
                shrink = jnp.exp2(before - now)
                weight = jnp.exp2(score - wide(now, keys)).astype(BF16)
                added = jnp.dot(
                    weight, jnp.concatenate([value, jnp.ones_like(value)], axis=1), preferred_element_type=F32
                )
                acc[j, rows, :] = acc[j, rows, :] * wide(shrink, 256) + added
                top[j, rows, :] = now

    def partner_head(j):
        lanes = slice(j * 128, (j + 1) * 128)
        lane = lax.broadcasted_iota(jnp.int32, (step, 128), 1)
        for t in range(tiles):
            rows = slice(t * step, (t + 1) * step)
            query = qs[1, rows, lanes]
            factor = fac[1, rows, :]
            scores = [
                lax.dot_general(query, kvs[k, 0, :, lanes], (((1,), (1,)), ((), ())), preferred_element_type=F32)
                * wide(factor, 2 * tok)
                for k in range(4)
            ]
            highest = jnp.max(functools.reduce(jnp.maximum, scores), axis=1, keepdims=True)
            highest = jnp.broadcast_to(highest, (step, 128))
            summed = None
            for k in range(4):
                weight = jnp.exp2(scores[k] - wide(highest, 2 * tok)).astype(BF16)
                value = kvs[k, 1, :, lanes]
                added = jnp.dot(
                    weight, jnp.concatenate([value, jnp.ones_like(value)], axis=1), preferred_element_type=F32
                )
                summed = added if summed is None else summed + added
            total = summed[:, 128:]
            o_send[j, rows, :] = (summed[:, :128] / total).astype(BF16)
            lse[rows, :] = jnp.where(lane == j, highest + jnp.log2(total), lse[rows, :])

    weight_first(0)
    kv_out(0)
    weight_third(0)
    for m in (1, 2):
        weight_first(m)
        if SHARE3[m]:
            weight_third(m)

    loads[0].wait()

    def norm_rows(i, carry):
        rows = pl.ds(pl.multiple_of(i * 16, 16), 16)
        states = hid[rows, :].astype(F32)
        mean = jnp.mean(states, axis=1, keepdims=True)
        states = states - mean
        var = jnp.mean(states * states, axis=1, keepdims=True)
        nrm[rows, :] = (states * lax.rsqrt(var + 1e-06) * (1.0 + mod[1:2, :]) + mod[0:1, :]).astype(BF16)
        return carry

    lax.fori_loop(0, tok // 16, norm_rows, 0)

    for load in loads[1:4]:
        load.wait()
    own_lanes = pl.ds(pl.multiple_of(c * depth, 128), depth)

    def own_dot(m, carry):
        @pl.when(m == 1)
        def _():
            weight_on(0, 0)

        raw[m] = jnp.dot(nrm[:, own_lanes], wown[m], preferred_element_type=F32)
        return carry

    lax.fori_loop(0, 3, own_dot, 0)

    weight_on(0, 1)
    kv_out(1)
    top[...] = jnp.full_like(top, LOW)
    acc[...] = jnp.zeros_like(acc)
    lse[...] = jnp.zeros_like(lse)
    weight_dot(0, 0)
    weight_dot(0, 2)
    kv_forward(0)
    weight_rest(0)
    weight_dot(0, 1)
    weight_dot(0, 3)
    for j in range(heads):
        lanes = slice(j * 128, (j + 1) * 128)
        qs[0, :, lanes] = (raw[0, :, lanes] * head_gain(gain_q, j)).astype(BF16)
    send(qs.at[0], qs.at[1], qss.at[0], qsr.at[0], X2)
    pending(lambda: (qs.at[0], qss.at[0]))
    squares_out(0, 0)
    loads[4].wait()
    kv_ready(0)
    fac_rows[0] = norm_factor(0) * SCORE_SCALE
    send(fac_rows.at[0], fac_rows.at[1], qss.at[1], qsr.at[1], X2)
    pending(lambda: (fac_rows.at[0], qss.at[1]))
    spread(0)

    attend(kvs.at[0, 0, other], kvs.at[0, 1, other])
    kv_forward(1)

    def unit(i, carry):
        @pl.when(i == 0)
        def _():
            kv_ready(1)

        @pl.when(i == 1)
        def _():
            weight_on(1, 0)
            kv_ready(2)

        attend(kvs.at[i + 1, 0], kvs.at[i + 1, 1])
        return carry

    lax.fori_loop(0, 2, unit, 0)

    weight_on(1, 1)
    weight_dot(1, 0)
    weight_dot(1, 2)
    kv_last(0)
    kv_last(1)
    kv_ready(3)
    arrived(qs.at[1], qsr.at[0])
    arrived(fac_rows.at[1], qsr.at[1])
    spread(1)
    for j in range(heads):
        partner_head(j)
    for j in range(heads):
        send(o_send.at[j], o_recv.at[j], oss.at[j], osr.at[j], X2)
    lse_send[...] = jnp.transpose(lse[...])[:8, :]
    send(lse_send, lse_recv, oss.at[heads], osr.at[heads], X2)
    weight_on(2, 0)
    weight_on(2, 1)
    weight_rest(1)
    weight_dot(1, 1)
    weight_dot(1, 3)
    squares_out(1, 1)
    attend(kvs.at[3, 0], kvs.at[3, 1])
    for j in range(heads):
        pending(lambda j=j: (o_send.at[j], oss.at[j]))
    pending(lambda: (lse_send, oss.at[heads]))

    weight_dot(2, 0)
    weight_dot(2, 2)
    factors = norm_factor(1)
    for i in range(blocks):
        rows = slice(i * 128, (i + 1) * 128)
        factor = column_of(factors, i)
        for j in range(heads):
            lanes = slice(j * 128, (j + 1) * 128)
            fresh[0, 0, rows, lanes] = (raw[1, rows, lanes] * factor * head_gain(gain_k, j)).astype(BF16)
    results = [
        pltpu.make_async_copy(fresh.at[0, 0], fresh_out.at[0, 0], ld.at[0]),
        pltpu.make_async_copy(fresh.at[0, 1], fresh_out.at[0, 1], ld.at[1]),
        pltpu.make_async_copy(att, att_out, ld.at[2]),
    ]
    results[0].start()
    weight_rest(2)
    weight_dot(2, 1)
    weight_dot(2, 3)
    fresh[0, 1] = raw[2].astype(BF16)
    results[1].start()
    attend(fresh.at[0, 0], fresh.at[0, 1])

    for j in range(heads):
        arrived(o_recv.at[j], osr.at[j])
    arrived(lse_recv, osr.at[heads])
    far = jnp.transpose(jnp.concatenate([lse_recv[...]] * 16, axis=0))
    for j in range(heads):
        near = top[j]
        there = jnp.broadcast_to(far[:, j : j + 1], (tok, 128))
        highest = jnp.maximum(near, there)
        a = jnp.exp2(near - highest)
        b = jnp.exp2(there - highest)
        summed = acc[j, :, :128] * a + o_recv[j].astype(F32) * b
        att[0, :, j * 128 : (j + 1) * 128] = (summed / (acc[j, :, 128:] * a + b)).astype(BF16)
    results[2].start()

    for describe in sent:
        src, ss = describe()
        pltpu.make_async_remote_copy(
            src_ref=src, dst_ref=src, send_sem=ss, recv_sem=ss, device_id=SIB, device_id_type=MESH
        ).wait_send()
    for result in results:
        result.wait()


def hand_over(att_in, fresh_in, att_out, fresh_out, att, fresh, sem):
    tiles = [
        (fresh_in.at[0, 0], fresh.at[0, 0], fresh_out.at[0, 0]),
        (fresh_in.at[0, 1], fresh.at[0, 1], fresh_out.at[0, 1]),
        (att_in, att, att_out),
    ]
    come = [pltpu.make_async_copy(src, held, sem.at[0, i]) for i, (src, held, _) in enumerate(tiles)]
    go = [pltpu.make_async_copy(held, dst, sem.at[1, i]) for i, (_, held, dst) in enumerate(tiles)]
    for copy in come:
        copy.start()
    for first, second in zip(come, go):
        first.wait()
        second.start()
    for copy in go:
        copy.wait()


def local(n_head, hidden_states, modulation, w_query, w_key, w_value, query_gain, key_gain, stale_kv):
    tok = hidden_states.shape[1]
    depth, width = w_query.shape
    heads = width // HEAD_DIM
    hbm = pl.BlockSpec(memory_space=pl.ANY)
    vmem = pl.BlockSpec(memory_space=pltpu.VMEM)
    dma = pltpu.SemaphoreType.DMA
    peers = max(n_head - 1, 1)
    shapes = (
        jax.ShapeDtypeStruct((1, tok, width), BF16),
        jax.ShapeDtypeStruct((1, 2, tok, width), BF16),
    )
    results = pl.pallas_call(
        functools.partial(kernel, n_head, float(n_head * width)),
        out_shape=shapes,
        in_specs=[hbm, vmem, hbm, hbm, hbm, vmem, vmem, hbm],
        out_specs=(hbm, hbm),
        scratch_shapes=[
            pltpu.VMEM((1, tok, width), BF16),
            pltpu.VMEM((1, 2, tok, width), BF16),
            pltpu.VMEM((tok, 2 * depth), BF16),
            pltpu.VMEM((tok, 2 * depth), BF16),
            pltpu.VMEM((3, depth, width), BF16),
            pltpu.VMEM((3, depth, width), BF16),
            pltpu.VMEM((3, tok, width), F32),
            pltpu.VMEM((4, 2, 2 * tok, width), BF16),
            pltpu.VMEM((2, tok, width), BF16),
            pltpu.VMEM((2, tok, 128), F32),
            pltpu.VMEM((2, 8, 128), F32),
            pltpu.VMEM((heads, tok, 128), F32),
            pltpu.VMEM((heads, tok, 256), F32),
            pltpu.VMEM((heads, tok, 128), BF16),
            pltpu.VMEM((heads, tok, 128), BF16),
            pltpu.VMEM((tok, 128), F32),
            pltpu.VMEM((8, tok), F32),
            pltpu.VMEM((8, tok), F32),
            pltpu.VMEM((2, n_head, 8, 128), F32),
            dma((5,)),
            dma((3, 4, 2)), dma((3, 4, 2)), dma((3, 4, 2)), dma((3, 4, 2)),
            dma((2, 2)), dma((2, 2)), dma((2, 2)), dma((2, 2)), dma((4, 2)), dma((4, 2)),
            dma((2,)), dma((2,)), dma((heads + 1,)), dma((heads + 1,)), dma((2, peers)), dma((2, peers)),
        ],
        compiler_params=pltpu.CompilerParams(
            collective_id=0, has_side_effects=True, vmem_limit_bytes=60 * 2**20
        ),
    )(
        hidden_states, modulation, w_query, w_key, w_value,
        query_gain, key_gain, stale_kv,
    )
    return pl.pallas_call(
        hand_over,
        out_shape=shapes,
        in_specs=[hbm, hbm],
        out_specs=(hbm, hbm),
        scratch_shapes=[
            pltpu.VMEM((1, tok, width), BF16),
            pltpu.VMEM((1, 2, tok, width), BF16),
            dma((2, 3)),
        ],
    )(*results)


def solution(mesh):
    in_specs = (
        P("cfg", "patch", None),
        P(),
        P("cfg", "head"),
        P("cfg", "head"),
        P("cfg", "head"),
        P("head"),
        P("head"),
        P("cfg", None, "patch", "head"),
    )
    out_specs = (P("cfg", "patch", "head"), P("cfg", None, "patch", "head"))
    run = functools.partial(local, mesh.shape["head"])
    return jax.shard_map(run, mesh=mesh, in_specs=in_specs, out_specs=out_specs, check_vma=False)
```

time: 95.6 us -> 84.1 us (0.88)
  the two profiles are of different devices: /device:TPU:2 before, /device:TPU:1 now
where the time goes in v2:
time: 84.1 us; the launch traced here: 83.9 us
  Pallas kernels  83.1 us (99%)
    pallas_call x1, Pallas kernels, local(): pl.pallas_call(functools.partial(kernel, n_head, float(n_head * width)),...  80.9 us
    pallas_call x1, Pallas kernels, local(): pl.pallas_call(hand_over, out_shape=shapes, in_specs=[hbm, hbm], out_spec...  2.18 us

profile of v2, /device:TPU:1, one launch (start us, length us, event | category | flops | bytes accessed | tf_op | source)
XLA Modules:
  0.0 83.9 jit_solution(1717529700056947671)
XLA Ops:
  0.6 80.9 %shard_map.95 = (bf16[1,384,640]{2,1,0:T(8,128)(2,1)}, bf16[1,2,384,640]{3,2,1,0:T(8,128)(2,1)}) custom-call(bf16[1,384,5120]{2,1,0:T(8,128)(2,1)} %hid_any.1, f32[2,5120]{1,0:T(2,128)} %mod.1, bf16[2560,640]{1,0:T(8,128)(2,1)} %wq_any.1, bf16[2560,640]{1,0:T(8,128)(2,1)} %wk_any.1, bf16[2560,640]{1,0:T(8,128)(2,1)} %wv_any.1, f32[640]{0:T(1024)} %gain_q.1, ...), custom_call_target="tpu_custom_call" | custom-call | tf_op jit(solution)/shard_map/pallas_call | solution.py:435
  81.5 2.2 %shard_map.96 = (bf16[1,384,640]{2,1,0:T(8,128)(2,1)}, bf16[1,2,384,640]{3,2,1,0:T(8,128)(2,1)}) custom-call(bf16[1,384,640]{2,1,0:T(8,128)(2,1)} %get-tuple-element.4.att_in, bf16[1,2,384,640]{3,2,1,0:T(8,128)(2,1)} %get-tuple-element.5.fresh_in), custom_call_target="tpu_custom_call" | custom-call | tf_op jit(solution)/shard_map/pallas_call | solution.py:472

commit v3 on v2

--- a/solution.py
+++ b/solution.py
@@ -20,7 +20,7 @@
     n_head, columns_all,
     hid_any, mod, wq_any, wk_any, wv_any, gain_q, gain_k, stale_any,
     att_out, fresh_out,
-    att, fresh, hid, nrm, wown, woth, raw, kvs, qs, fac, fac_rows, top, acc, o_send, o_recv, lse, lse_send, lse_recv, zs,
+    att, fresh, hid, nrm, wown, woth, raw, kvs, qs, top, acc, o_send, o_recv, lse, lse_send, lse_recv, zs,
     ld, wps, wpr, wss, wsr, kys, kyr, k3s, k3r, kss, ksr, qss, qsr, oss, osr, zss, zsr,
 ):
     tok = hid.shape[0]
@@ -194,13 +194,17 @@
     def column_of(rows, i):
         return jnp.transpose(jnp.broadcast_to(rows[i : i + 1, :], (128, 128)))
 
-    def spread(s):
-        rows = fac_rows[s]
-        for i in range(blocks):
-            fac[s, i * 128 : (i + 1) * 128, :] = column_of(rows, i)
-
     def head_gain(gain, j):
         return gain[j * 128 : (j + 1) * 128][None, :]
+
+    def normalise(k, m, gain, out):
+        factors = norm_factor(k)
+        for i in range(blocks):
+            rows = slice(i * 128, (i + 1) * 128)
+            factor = column_of(factors, i)
+            for j in range(heads):
+                lanes = slice(j * 128, (j + 1) * 128)
+                out[rows, lanes] = (raw[m, rows, lanes] * factor * head_gain(gain, j)).astype(BF16)
 
     def wide(v, keys):
         return jnp.concatenate([v] * (keys // 128), axis=1)
@@ -218,7 +222,7 @@
                 score = lax.dot_general(
                     qs[0, rows, lanes], key_ref[:, lanes], (((1,), (1,)), ((), ())), preferred_element_type=F32
                 )
-                score = score * wide(fac[0, rows, :], keys)
+                score = score * SCORE_SCALE
                 before = top[j, rows, :]
                 now = jnp.maximum(before, jnp.max(score, axis=1, keepdims=True))
                 shrink = jnp.exp2(before - now)
@@ -235,10 +239,9 @@
         for t in range(tiles):
             rows = slice(t * step, (t + 1) * step)
             query = qs[1, rows, lanes]
-            factor = fac[1, rows, :]
             scores = [
                 lax.dot_general(query, kvs[k, 0, :, lanes], (((1,), (1,)), ((), ())), preferred_element_type=F32)
-                * wide(factor, 2 * tok)
+                * SCORE_SCALE
                 for k in range(4)
             ]
             highest = jnp.max(functools.reduce(jnp.maximum, scores), axis=1, keepdims=True)
@@ -301,18 +304,12 @@
     weight_rest(0)
     weight_dot(0, 1)
     weight_dot(0, 3)
-    for j in range(heads):
-        lanes = slice(j * 128, (j + 1) * 128)
-        qs[0, :, lanes] = (raw[0, :, lanes] * head_gain(gain_q, j)).astype(BF16)
-    send(qs.at[0], qs.at[1], qss.at[0], qsr.at[0], X2)
-    pending(lambda: (qs.at[0], qss.at[0]))
     squares_out(0, 0)
     loads[4].wait()
     kv_ready(0)
-    fac_rows[0] = norm_factor(0) * SCORE_SCALE
-    send(fac_rows.at[0], fac_rows.at[1], qss.at[1], qsr.at[1], X2)
-    pending(lambda: (fac_rows.at[0], qss.at[1]))
-    spread(0)
+    normalise(0, 0, gain_q, qs.at[0])
+    send(qs.at[0], qs.at[1], qss.at[0], qsr.at[0], X2)
+    pending(lambda: (qs.at[0], qss.at[0]))
 
     attend(kvs.at[0, 0, other], kvs.at[0, 1, other])
     kv_forward(1)
@@ -339,16 +336,18 @@
     kv_last(1)
     kv_ready(3)
     arrived(qs.at[1], qsr.at[0])
-    arrived(fac_rows.at[1], qsr.at[1])
-    spread(1)
-    for j in range(heads):
+    weight_on(2, 0)
+    for j in range(min(3, heads)):
         partner_head(j)
-    for j in range(heads):
+    for j in range(min(3, heads)):
+        send(o_send.at[j], o_recv.at[j], oss.at[j], osr.at[j], X2)
+    weight_on(2, 1)
+    for j in range(3, heads):
+        partner_head(j)
+    for j in range(3, heads):
         send(o_send.at[j], o_recv.at[j], oss.at[j], osr.at[j], X2)
     lse_send[...] = jnp.transpose(lse[...])[:8, :]
     send(lse_send, lse_recv, oss.at[heads], osr.at[heads], X2)
-    weight_on(2, 0)
-    weight_on(2, 1)
     weight_rest(1)
     weight_dot(1, 1)
     weight_dot(1, 3)
@@ -360,13 +359,7 @@
 
     weight_dot(2, 0)
     weight_dot(2, 2)
-    factors = norm_factor(1)
-    for i in range(blocks):
-        rows = slice(i * 128, (i + 1) * 128)
-        factor = column_of(factors, i)
-        for j in range(heads):
-            lanes = slice(j * 128, (j + 1) * 128)
-            fresh[0, 0, rows, lanes] = (raw[1, rows, lanes] * factor * head_gain(gain_k, j)).astype(BF16)
+    normalise(1, 1, gain_k, fresh.at[0, 0])
     results = [
         pltpu.make_async_copy(fresh.at[0, 0], fresh_out.at[0, 0], ld.at[0]),
         pltpu.make_async_copy(fresh.at[0, 1], fresh_out.at[0, 1], ld.at[1]),
@@ -447,8 +440,6 @@
             pltpu.VMEM((3, tok, width), F32),
             pltpu.VMEM((4, 2, 2 * tok, width), BF16),
             pltpu.VMEM((2, tok, width), BF16),
-            pltpu.VMEM((2, tok, 128), F32),
-            pltpu.VMEM((2, 8, 128), F32),
             pltpu.VMEM((heads, tok, 128), F32),
             pltpu.VMEM((heads, tok, 256), F32),
             pltpu.VMEM((heads, tok, 128), BF16),
@@ -460,7 +451,7 @@
             dma((5,)),
             dma((3, 4, 2)), dma((3, 4, 2)), dma((3, 4, 2)), dma((3, 4, 2)),
             dma((2, 2)), dma((2, 2)), dma((2, 2)), dma((2, 2)), dma((4, 2)), dma((4, 2)),
-            dma((2,)), dma((2,)), dma((heads + 1,)), dma((heads + 1,)), dma((2, peers)), dma((2, peers)),
+            dma((1,)), dma((1,)), dma((heads + 1,)), dma((heads + 1,)), dma((2, peers)), dma((2, peers)),
         ],
         compiler_params=pltpu.CompilerParams(
             collective_id=0, has_side_effects=True, vmem_limit_bytes=60 * 2**20

time: 84.1 us -> 79.9 us (0.950)
  Pallas kernels: 83.1 us -> 78.9 us
    pallas_call x1, Pallas kernels: 80.9 us -> 76.7 us  [local(): pl.pallas_call(functools.partial(kernel, n_head, float(n_head * width)),...]
where the time goes in v3:
time: 79.9 us; the launch traced here: 79.7 us
  Pallas kernels  78.9 us (99%)
  between operations  0.82 us (1%)
    pallas_call x1, Pallas kernels, local(): pl.pallas_call(functools.partial(kernel, n_head, float(n_head * width)),...  76.7 us
    pallas_call x1, Pallas kernels, local(): pl.pallas_call(hand_over, out_shape=shapes, in_specs=[hbm, hbm], out_spec...  2.18 us

profile of v3, /device:TPU:1, one launch (start us, length us, event | category | flops | bytes accessed | tf_op | source)
XLA Modules:
  0.0 79.7 jit_solution(8842290844438228264)
XLA Ops:
  0.6 76.7 %shard_map.95 = (bf16[1,384,640]{2,1,0:T(8,128)(2,1)}, bf16[1,2,384,640]{3,2,1,0:T(8,128)(2,1)}) custom-call(bf16[1,384,5120]{2,1,0:T(8,128)(2,1)} %hid_any.1, f32[2,5120]{1,0:T(2,128)} %mod.1, bf16[2560,640]{1,0:T(8,128)(2,1)} %wq_any.1, bf16[2560,640]{1,0:T(8,128)(2,1)} %wk_any.1, bf16[2560,640]{1,0:T(8,128)(2,1)} %wv_any.1, f32[640]{0:T(1024)} %gain_q.1, ...), custom_call_target="tpu_custom_call" | custom-call | tf_op jit(solution)/shard_map/pallas_call | solution.py:428
  77.3 2.2 %shard_map.96 = (bf16[1,384,640]{2,1,0:T(8,128)(2,1)}, bf16[1,2,384,640]{3,2,1,0:T(8,128)(2,1)}) custom-call(bf16[1,384,640]{2,1,0:T(8,128)(2,1)} %get-tuple-element.4.att_in, bf16[1,2,384,640]{3,2,1,0:T(8,128)(2,1)} %get-tuple-element.5.fresh_in), custom_call_target="tpu_custom_call" | custom-call | tf_op jit(solution)/shard_map/pallas_call | solution.py:463

commit v4 on v3

--- a/solution.py
+++ b/solution.py
@@ -335,6 +335,7 @@
     kv_last(0)
     kv_last(1)
     kv_ready(3)
+    attend(kvs.at[3, 0], kvs.at[3, 1])
     arrived(qs.at[1], qsr.at[0])
     weight_on(2, 0)
     for j in range(min(3, heads)):
@@ -352,7 +353,6 @@
     weight_dot(1, 1)
     weight_dot(1, 3)
     squares_out(1, 1)
-    attend(kvs.at[3, 0], kvs.at[3, 1])
     for j in range(heads):
         pending(lambda j=j: (o_send.at[j], oss.at[j]))
     pending(lambda: (lse_send, oss.at[heads]))

time: 79.9 us -> 81.5 us (1.020)
  Pallas kernels: 78.9 us -> 80.5 us
    pallas_call x1, Pallas kernels: 76.7 us -> 78.3 us  [local(): pl.pallas_call(functools.partial(kernel, n_head, float(n_head * width)),...]
where the time goes in v4:
time: 81.5 us; the launch traced here: 81.3 us
  Pallas kernels  80.5 us (99%)
  between operations  0.82 us (1%)
    pallas_call x1, Pallas kernels, local(): pl.pallas_call(functools.partial(kernel, n_head, float(n_head * width)),...  78.3 us
    pallas_call x1, Pallas kernels, local(): pl.pallas_call(hand_over, out_shape=shapes, in_specs=[hbm, hbm], out_spec...  2.18 us

profile of v4, /device:TPU:1, one launch (start us, length us, event | category | flops | bytes accessed | tf_op | source)
XLA Modules:
  0.0 81.3 jit_solution(8091616674645975672)
XLA Ops:
  0.6 78.3 %shard_map.95 = (bf16[1,384,640]{2,1,0:T(8,128)(2,1)}, bf16[1,2,384,640]{3,2,1,0:T(8,128)(2,1)}) custom-call(bf16[1,384,5120]{2,1,0:T(8,128)(2,1)} %hid_any.1, f32[2,5120]{1,0:T(2,128)} %mod.1, bf16[2560,640]{1,0:T(8,128)(2,1)} %wq_any.1, bf16[2560,640]{1,0:T(8,128)(2,1)} %wk_any.1, bf16[2560,640]{1,0:T(8,128)(2,1)} %wv_any.1, f32[640]{0:T(1024)} %gain_q.1, ...), custom_call_target="tpu_custom_call" | custom-call | tf_op jit(solution)/shard_map/pallas_call | solution.py:428
  79.0 2.2 %shard_map.96 = (bf16[1,384,640]{2,1,0:T(8,128)(2,1)}, bf16[1,2,384,640]{3,2,1,0:T(8,128)(2,1)}) custom-call(bf16[1,384,640]{2,1,0:T(8,128)(2,1)} %get-tuple-element.4.att_in, bf16[1,2,384,640]{3,2,1,0:T(8,128)(2,1)} %get-tuple-element.5.fresh_in), custom_call_target="tpu_custom_call" | custom-call | tf_op jit(solution)/shard_map/pallas_call | solution.py:463
